TPU v7x, 32 devices: a whole 2x2x4 slice. The times are simulated.
32 devices in a mesh: parts: 1, fsdp: 8 (over z, y), query: 4 (over x, core).
Axes of the slice: x: 2, y: 2, z: 4, core: 2. Of those that a mesh axis runs over, the one named last changes fastest.
Arguments:
- resid_in: bfloat16 [2048, 8192], P(('parts', 'fsdp'), 'query'), may hold values from -120 to 120
- resid_grad: bfloat16 [2048, 8192], P(('parts', 'fsdp'), 'query'), may hold values from -6 to 6
- query_path_grad: bfloat16 [2048, 8192], P(('parts', 'fsdp'), 'query'), may hold values from -6 to 6
- hidden_act: bfloat16 [2048, 28672], P(('parts', 'fsdp'), 'query'), may hold values from -6 to 6
- key_grad: bfloat16 [2048, 1024], P(('parts', 'fsdp'), 'query'), may hold values from -6 to 6
- value_grad: bfloat16 [2048, 1024], P(('parts', 'fsdp'), 'query'), may hold values from -6 to 6
- key_weight: bfloat16 [8192, 1024], P('query', 'fsdp'), may hold values from -0.171875 to 0.171875
- value_weight: bfloat16 [8192, 1024], P('query', 'fsdp'), may hold values from -0.171875 to 0.171875
- norm_gain: bfloat16 [8192], P('query'), may hold values from 0.099609375 to 1.8984375
- proj_attn_in: bfloat16 [64, 8192], P(None, 'query'), may hold values from -0.0625 to 0.0625
- proj_key_out: bfloat16 [64, 1024], P(None, 'query'), may hold values from -0.1875 to 0.1875
- proj_value_out: bfloat16 [64, 1024], P(None, 'query'), may hold values from -0.1875 to 0.1875
- proj_down_in: bfloat16 [64, 28672], P(None, 'query'), may hold values from -0.03125 to 0.03125
- proj_down_out: bfloat16 [64, 8192], P(None, 'query'), may hold values from -0.0625 to 0.0625
- query_grads: bfloat16 [4096, 12288], P(('fsdp', 'query')), may hold values from -0.0012207031 to 0.0012207031
- seq_counts: int32 [1], P('parts'), may hold values from 256 to 2048, as said below
Outputs:
- scores: float32 [1, 4096], P('parts', ('fsdp', 'query'))
Inputs may be any that keep to these rules, and one draw needn't show every extreme that they name: `seq_counts`: in every part at least one sequence has all 2048 positions valid.
All inputs are finite; a program needn't handle non-finite values.
Results may differ from a plain program's by a relative error of at most 0.0019.
Values may be sent and summed in bfloat16 or wider, within the bound.
A program may use at most 64 MiB of HBM per device.

v0:
```python
import jax
import jax.numpy as jnp
from jax import lax
from jax.sharding import PartitionSpec as P

D = 8192
LEN = 2048


def contract_last(left, right):
    return lax.dot_general(
        left, right, (((1,), (1,)), ((), ())), preferred_element_type=jnp.float32
    )


def gram_blocks(weights_mask, outer_rows, inner_rows):
    count, groups = weights_mask.shape
    width = outer_rows.shape[1]
    scaled = (weights_mask[:, :, None] * outer_rows[:, None, :]).reshape(count, groups * width)
    block = jnp.dot(
        scaled.T, inner_rows, precision=lax.Precision.HIGHEST, preferred_element_type=jnp.float32
    )
    return block.reshape(groups, width * inner_rows.shape[1])


def shards(
    resid_in,
    resid_grad,
    query_path_grad,
    hidden_act,
    key_grad,
    value_grad,
    key_weight,
    value_weight,
    norm_gain,
    proj_attn_in,
    proj_key_out,
    proj_value_out,
    proj_down_in,
    proj_down_out,
    query_grads,
    seq_counts,
):
    tok_rows = resid_in.shape[0]
    fsdp_place = lax.axis_index("fsdp")
    key_whole, value_whole = (
        lax.all_gather(key_grad, "query", axis=1, tiled=True),
        lax.all_gather(value_grad, "query", axis=1, tiled=True),
    )
    early = jnp.concatenate(
        [
            contract_last(key_grad, proj_key_out),
            contract_last(value_grad, proj_value_out),
            contract_last(hidden_act, proj_down_in),
        ],
        axis=1,
    )
    resid_f = resid_in.astype(jnp.float32)
    sum_squares, early = lax.psum((jnp.sum(resid_f * resid_f, axis=1), early), "query")
    inv_rms = lax.rsqrt(sum_squares / D + 1e-05)
    gain_f = norm_gain.astype(jnp.float32)
    normed = (resid_f * inv_rms[:, None] * gain_f).astype(jnp.bfloat16)
    attn_in = contract_last(normed, proj_attn_in)
    initial = query_path_grad.astype(jnp.float32)
    columns = key_whole
    input_grad = initial + contract_last(
        columns, lax.all_gather(key_weight, "fsdp", axis=1, tiled=True)
    )
    columns = value_whole
    input_grad = input_grad + contract_last(
        columns, lax.all_gather(value_weight, "fsdp", axis=1, tiled=True)
    )
    scaled_grad = gain_f * input_grad
    dot_part = jnp.sum(resid_f * scaled_grad, axis=1) / D
    down_proj_f = proj_down_out.astype(jnp.float32)
    mean_dot, attn_in = lax.psum((dot_part, attn_in), "query")
    cubed = inv_rms * inv_rms * inv_rms * mean_dot
    resid_back = (
        resid_grad.astype(jnp.float32) + inv_rms[:, None] * scaled_grad - resid_f * cubed[:, None]
    )
    down_part = jnp.dot(
        resid_back,
        down_proj_f.T,
        precision=lax.Precision.HIGHEST,
        preferred_element_type=jnp.float32,
    )
    down_out = lax.psum(down_part, "query")
    width = proj_attn_in.shape[0]
    key_out = early[:, :width]
    value_out = early[:, width : 2 * width]
    hidden_in = early[:, 2 * width :]
    seq_total = seq_counts.shape[0]
    positions = fsdp_place * tok_rows + lax.iota(jnp.int32, tok_rows)
    seq_index = positions // LEN
    offset = positions % LEN
    onehot = seq_index[:, None] == lax.iota(jnp.int32, seq_total)[None, :]
    limit = jnp.sum(jnp.where(onehot, seq_counts[None, :], 0), axis=1)
    weights_mask = jnp.where(onehot & (offset < limit)[:, None], 1.0, 0.0).astype(jnp.float32)
    local = jnp.concatenate(
        [
            gram_blocks(weights_mask, key_out, attn_in),
            gram_blocks(weights_mask, value_out, attn_in),
            gram_blocks(weights_mask, down_out, hidden_in),
        ],
        axis=1,
    )
    seq_grad = lax.psum(local, "fsdp")
    return jnp.dot(
        seq_grad,
        query_grads.astype(jnp.float32).T,
        precision=lax.Precision.HIGHEST,
        preferred_element_type=jnp.float32,
    )


def solution(mesh):
    placed = (
        P(("parts", "fsdp"), "query"),
        P(("parts", "fsdp"), "query"),
        P(("parts", "fsdp"), "query"),
        P(("parts", "fsdp"), "query"),
        P(("parts", "fsdp"), "query"),
        P(("parts", "fsdp"), "query"),
        P("query", "fsdp"),
        P("query", "fsdp"),
        P("query"),
        P(None, "query"),
        P(None, "query"),
        P(None, "query"),
        P(None, "query"),
        P(None, "query"),
        P(("fsdp", "query"), None),
        P("parts"),
    )
    return jax.shard_map(
        shards, mesh=mesh, in_specs=placed, out_specs=P("parts", ("fsdp", "query")), check_vma=False
    )
```

profile of v0, /device:TPU:0, one launch (start us, length us, event | category | flops | bytes accessed | tf_op | source)
XLA Modules:
  0.0 262.5 jit_solution(1866814675767182510)
XLA Ops:
  6.5 0.0 copy-start
  6.5 0.0 all-gather.3.cloned.1.call-start
  6.5 0.7 all-gather.3.cloned.1.call-update
  7.3 0.0 all-gather.5.cloned.1.call-start
  7.3 0.7 all-gather.5.cloned.1.call-update
  8.0 0.0 all-reduce.4.cloned.1.call-start
  8.1 0.7 convert_element_type.18
  8.7 1.1 fusion.26
  9.8 1.1 fusion.27
  10.9 0.0 copy-start.3
  10.9 3.6 %fusion.28 = f32[256,64]{0,1:T(8,128)S(1)} fusion(bf16[256,7168]{1,0:T(8,128)(2,1)} %param.19, bf16[64,7168]{1,0:T(8,128)(2,1)} %param.28), kind=kOutput, calls=%fused_computation.45 | convolution fusion | flops 234881024 | bytes 4653056 | tf_op jit(solution)/shard_map/dot_general | solution.py:11
  14.5 0.7 pad_maximum_fusion
  15.2 0.0 copy-done.2
  15.2 9.1 %all_gather.12 = bf16[256,1024]{1,0:T(8,128)(2,1)} all-gather(bf16[256,256]{1,0:T(8,128)(2,1)S(1)} %copy-done.2), channel_id=1, replica_groups=mesh['parts'=1,'fsdp'=8,'query'=4] {'query'}, dimensions={1}, use_global_device_ids=true | all-gather | bytes 655360 | tf_op jit(solution)/shard_map/all_gather | solution.py:47
  24.3 7.7 %all_gather.14 = bf16[256,1024]{1,0:T(8,128)(2,1)} all-gather(bf16[256,256]{1,0:T(8,128)(2,1)S(1)} %copy-done.3), channel_id=1, replica_groups=mesh['parts'=1,'fsdp'=8,'query'=4] {'query'}, dimensions={1}, use_global_device_ids=true | all-gather | bytes 655360 | tf_op jit(solution)/shard_map/all_gather | solution.py:48
  32.0 55.1 %all-gather.3.cloned.1.call-done = bf16[2048,1024]{1,0:T(8,128)(2,1)} async-done(((bf16[2048,128]{1,0:T(8,128)(2,1)}), bf16[2048,1024]{1,0:T(8,128)(2,1)}) %all-gather.3.cloned.1.call-update) | async-done | bytes 4194320 | tf_op jit(solution)/shard_map/all_gather | solution.py:67
  87.2 5.3 %convolution_add_fusion.1 = f32[256,2048]{1,0:T(8,128)} fusion(bf16[256,1024]{1,0:T(8,128)(2,1)} %all_gather.12, bf16[2048,1024]{1,0:T(8,128)(2,1)} %all-gather.3.cloned.1.call-done, bf16[256,2048]{1,0:T(8,128)(2,1)} %param.18), kind=kOutput, calls=%fused_computation.6 | convolution fusion | flops 1074790400 | bytes 7864320 | tf_op jit(solution)/shard_map/dot_general | solution.py:11
  92.4 70.0 %all-gather.5.cloned.1.call-done = bf16[2048,1024]{1,0:T(8,128)(2,1)} async-done(((bf16[2048,128]{1,0:T(8,128)(2,1)}), bf16[2048,1024]{1,0:T(8,128)(2,1)}) %all-gather.5.cloned.1.call-update) | async-done | bytes 4194320 | tf_op jit(solution)/shard_map/all_gather | solution.py:71
  162.4 6.2 %fusion.1 = (f32[256]{0:T(256)S(1)}, f32[256]{0:T(256)S(1)}, f32[256,2048]{1,0:T(8,128)}) fusion(bf16[256,2048]{1,0:T(8,128)(2,1)} %param.16, f32[256,2048]{1,0:T(8,128)} %convolution_add_fusion.1, bf16[256,1024]{1,0:T(8,128)(2,1)} %all_gather.14, bf16[2048,1024]{1,0:T(8,128)(2,1)} %all-gather.5.cloned.1.call-done, f32[2048]{0:T(1024)S(1)} %convert_element_type.18), kind=kOutput, calls=%fused_computation.7 | convolution fusion | flops 1077411328 | bytes 9971712 | tf_op jit(solution)/shard_map/dot_general | solution.py:11
  168.6 6.1 %all-reduce = (f32[256]{0:T(256)S(1)}, f32[256]{0:T(256)S(1)}) all-reduce(f32[256]{0:T(256)S(1)} %broadcast_multiply_fusion, f32[256]{0:T(256)S(1)} %get-tuple-element.5), channel_id=1, replica_groups=mesh['parts'=1,'fsdp'=8,'query'=4] {'query'}, use_global_device_ids=true, to_apply=%region_5.0 | all-reduce | flops 512 | bytes 4096 | tf_op jit(solution)/shard_map/psum | solution.py:76
  174.8 2.5 fusion.11
  177.3 3.8 %fusion.6 = f32[256,64]{0,1:T(8,128)} fusion(bf16[64,2048]{1,0:T(8,128)(2,1)S(1)} %copy-done.4, bf16[256,2048]{1,0:T(8,128)(2,1)} %param.16, f32[256,2048]{1,0:T(8,128)S(1)} %copy-done.1, bf16[256,2048]{1,0:T(8,128)(2,1)} %param.17, f32[256]{0:T(256)S(1)} %get-tuple-element.13, f32[256]{0:T(256)S(1)} %get-tuple-element.12), kind=kOutput, calls=%fused_computation.12 | convolution fusion | flops 405798912 | bytes 4524032 | tf_op jit(solution)/shard_map/dot_general | solution.py:81
  181.1 0.0 all-reduce.4.cloned.1.call-update
  181.8 30.0 %all-reduce.4.cloned.1.call-done = (f32[256,192]{0,1:T(8,128)}, f32[256,64]{0,1:T(8,128)}, f32[256,64]{0,1:T(8,128)}) async-done(((f32[256,192]{0,1:T(8,128)}, f32[256,64]{0,1:T(8,128)}, f32[256,64]{0,1:T(8,128)}), (f32[256,192]{0,1:T(8,128)}, f32[256,64]{0,1:T(8,128)}, f32[256,64]{0,1:T(8,128)})) %all-reduce.4.cloned.1.call-update) | async-done | bytes 327696 | tf_op jit(solution)/shard_map/psum | solution.py:59
  211.8 1.1 fusion.20
  212.9 1.1 fusion.19
  214.0 0.1 reshape.72
  214.1 0.1 reshape.73
  214.2 1.1 fusion.17
  215.3 0.1 reshape.74
  215.4 37.5 %psum.47 = f32[12288]{0:T(1024)S(1)} all-reduce(f32[12288]{0:T(1024)S(1)} %bitcast.21), channel_id=1, replica_groups=mesh['parts'=1,'fsdp'=8,'query'=4] {'fsdp'}, use_global_device_ids=true, to_apply=%region_7.8 | all-reduce | flops 12288 | bytes 98304 | tf_op jit(solution)/shard_map/psum | solution.py:107
  252.9 3.1 %fusion.29 = f32[1,128]{1,0:T(1,128)} fusion(f32[12288,1]{0,1:T(1,128)S(1)} %bitcast.22, bf16[128,12288]{1,0:T(8,128)(2,1)S(1)} %copy-done), kind=kOutput, calls=%fused_computation.46 | convolution fusion | flops 18874368 | bytes 3195392 | tf_op jit(solution)/shard_map/dot_general | solution.py:108
  (11 shorter events, 0.1 us)
Async XLA Ops:
  6.5 246.4 %copy-start = (bf16[128,12288]{1,0:T(8,128)(2,1)S(1)}, bf16[128,12288]{1,0:T(8,128)(2,1)}, u32[]{:S(2)}) copy-start(bf16[128,12288]{1,0:T(8,128)(2,1)} %param.30) | copy-start | bytes 9437188
  6.5 80.6 %all-gather.3.cloned.1.call-start = ((), (), s32[]{:S(2)}) async-start(), calls=%async_computation | async-start | bytes 4718592 | tf_op jit(solution)/shard_map/all_gather | solution.py:67
  7.3 155.2 %all-gather.5.cloned.1.call-start = ((), (), s32[]{:S(2)}) async-start(), calls=%async_computation.1 | async-start | bytes 4718592 | tf_op jit(solution)/shard_map/all_gather | solution.py:71
  8.0 203.8 %all-reduce.4.cloned.1.call-start = ((), (), s32[]{:S(2)}) async-start(), calls=%async_computation.2 | async-start | bytes 655360 | tf_op jit(solution)/shard_map/psum | solution.py:59
  10.9 4.3 %copy-start.2 = (bf16[256,256]{1,0:T(8,128)(2,1)S(1)}, bf16[256,256]{1,0:T(8,128)(2,1)}, u32[]{:S(2)}) copy-start(bf16[256,256]{1,0:T(8,128)(2,1)} %param.20) | copy-start | bytes 393220
  10.9 13.4 %copy-start.3 = (bf16[256,256]{1,0:T(8,128)(2,1)S(1)}, bf16[256,256]{1,0:T(8,128)(2,1)}, u32[]{:S(2)}) copy-start(bf16[256,256]{1,0:T(8,128)(2,1)} %param.21) | copy-start | bytes 393220
  162.4 14.9 %copy-start.4 = (bf16[64,2048]{1,0:T(8,128)(2,1)S(1)}, bf16[64,2048]{1,0:T(8,128)(2,1)}, u32[]{:S(2)}) copy-start(bf16[64,2048]{1,0:T(8,128)(2,1)} %param.29) | copy-start | bytes 786436
  174.7 2.6 copy-start.1
Sparse Core Ops, SparseCore 0:
  9.4 77.7 all-gather.2
  89.2 73.1 all-gather.4
  181.2 30.5 all-reduce.3
where the time goes:
time: 263 us
  waiting for transfers between devices  157 us (60%)
  blocking collectives  60.5 us (23%)
  matrix products  29.8 us (11%)
  between operations  13.8 us (5%)
    all_gather x1, waiting for transfers between devices, shards(): lax.all_gather(value_weight, 'fsdp', axis=1, tiled=True)  70 us
    all_gather x1, waiting for transfers between devices, shards(): lax.all_gather(key_weight, 'fsdp', axis=1, tiled=True)  55.1 us
    psum x1, blocking collectives, shards(): seq_grad = lax.psum(local, 'fsdp')  37.5 us
    psum x1, waiting for transfers between devices, shards(): lax.psum((jnp.sum(resid_f * resid_f, axis=1), early), 'query')  30 us
    dot_general x6, matrix products, contract_last(): lax.dot_general(left, right, (((1,), (1,)), ((), ())), preferred_element_...  19.7 us
    all_gather x1, blocking collectives, shards(): lax.all_gather(key_grad, 'query', axis=1, tiled=True)  9.07 us
    all_gather x1, blocking collectives, shards(): lax.all_gather(value_grad, 'query', axis=1, tiled=True)  7.74 us
    psum x1, blocking collectives, shards(): mean_dot, attn_in = lax.psum((dot_part, attn_in), 'query')  6.13 us
  transfers between devices with their start and end apart: 3, of which 3 were waited for; matrix products, arithmetic and copies ran while one was open for 5% of the time, Pallas kernels for 0%

commit v1 on v0

v1 whole, which is shorter than its diff:
```python
import functools

import jax
import jax.numpy as jnp
from jax import lax
from jax.experimental import pallas as pl
from jax.experimental.pallas import tpu as pltpu
from jax.sharding import PartitionSpec as P

D = 8192
LEN = 2048
MESH = pl.DeviceIdType.MESH
F32 = jnp.float32
BF16 = jnp.bfloat16


def dot_nt(left, right):
    return lax.dot_general(left, right, (((1,), (1,)), ((), ())), preferred_element_type=F32)


def gram(left, right):
    return lax.dot_general(
        left,
        right,
        (((0,), (0,)), ((), ())),
        precision=lax.Precision.HIGHEST,
        preferred_element_type=F32,
    )


def split(value):
    high = value.astype(BF16)
    return high, (value - high.astype(F32)).astype(BF16)


def kernel(
    sizes,
    x_ref,
    rg_ref,
    qpg_ref,
    hid_ref,
    kg_ref,
    vg_ref,
    kgp_ref,
    w_ref,
    gain_ref,
    pai_ref,
    pko_ref,
    pvo_ref,
    pdi_ref,
    pdo_ref,
    mask_ref,
    out_kv,
    out_d,
    wg,
    xs,
    kgs,
    early,
    pks,
    prod,
    proj,
    kv_q,
    kv_f,
    d_q,
    d_f,
    w_recv,
    w_right,
    w_left,
    x_sem,
    kg_send,
    kg_recv,
    early_sem,
    pk_sem,
    kv_q_sem,
    kv_f_sem,
    d_q_sem,
    d_f_sem,
):
    F, Q, B, seqs = sizes
    A = F // B
    per_seq = F // seqs
    n = kgp_ref.shape[1]
    t, d = x_ref.shape
    r = pdo_ref.shape[0]
    f, q = lax.axis_index("fsdp"), lax.axis_index("query")
    a, b = f // B, lax.rem(f, B)

    barrier = pltpu.get_barrier_semaphore()
    others = 0
    for i in range(1, F):
        pl.semaphore_signal(
            barrier, inc=1, device_id={"fsdp": lax.rem(f + i, F)}, device_id_type=MESH
        )
        others += 1
    for bi in range(B):
        for qi in range(1, Q):
            pl.semaphore_signal(
                barrier,
                inc=1,
                device_id={"fsdp": a * B + lax.rem(b + bi, B), "query": lax.rem(q + qi, Q)},
                device_id_type=MESH,
            )
            others += 1
    pl.semaphore_wait(barrier, others)

    right = {"fsdp": jnp.minimum(f + B, F - 1 - lax.rem(F - 1 - f, B))}
    left = {"fsdp": jnp.maximum(f - B, b)}
    has_right, has_left = a < A - 1, a > 0

    def w_copy(src, slot, send, target):
        return pltpu.make_async_remote_copy(
            src_ref=src,
            dst_ref=wg.at[slot],
            send_sem=send.at[slot],
            recv_sem=w_recv.at[slot],
            device_id=target,
            device_id_type=MESH,
        )

    @pl.when(has_right)
    def _():
        w_copy(w_ref, a, w_right, right).start()

    @pl.when(has_left)
    def _():
        w_copy(w_ref, a, w_left, left).start()

    gain = gain_ref[...].astype(F32)
    own = pl.ds(pl.multiple_of(b * t, t), t)
    xs[own, :] = (x_ref[...].astype(F32) * gain).astype(BF16)
    gp_high, gp_low = split(pdo_ref[...].astype(F32) * gain)
    xs[pl.ds(B * t, r), :] = gp_high
    xs[pl.ds(B * t + r, r), :] = gp_low

    waits = []
    for bi in range(1, B):
        there = lax.rem(b + bi, B)
        copy = pltpu.make_async_remote_copy(
            src_ref=xs.at[own, :],
            dst_ref=xs.at[own, :],
            send_sem=x_sem.at[0, bi],
            recv_sem=x_sem.at[1, bi],
            device_id={"fsdp": a * B + there},
            device_id_type=MESH,
        )
        copy.start()
        waits.append(copy)
    kgs[pl.ds(q * n, n), own, :] = kgp_ref[b]
    for bi in range(B):
        for qi in range(Q):
            if bi == 0 and qi == 0:
                continue
            there = lax.rem(b + bi, B)
            copy = pltpu.make_async_remote_copy(
                src_ref=kgp_ref.at[there],
                dst_ref=kgs.at[pl.ds(q * n, n), own, :],
                send_sem=kg_send.at[bi, qi],
                recv_sem=kg_recv.at[bi, qi],
                device_id={"fsdp": a * B + there, "query": lax.rem(q + qi, Q)},
                device_id_type=MESH,
            )
            copy.start()
            waits.append(copy)

    def spread(buffer, sems, axis, me, count):
        copies = []
        for i in range(1, count):
            copy = pltpu.make_async_remote_copy(
                src_ref=buffer.at[me],
                dst_ref=buffer.at[me],
                send_sem=sems.at[0, i],
                recv_sem=sems.at[1, i],
                device_id={axis: lax.rem(me + i, count)},
                device_id_type=MESH,
            )
            copy.start()
            copies.append(copy)
        return copies

    x = x_ref[...]
    xf = x.astype(F32)
    early[q, :, pl.ds(0, r)] = dot_nt(kg_ref[...], pko_ref[...])
    early[q, :, pl.ds(r, r)] = dot_nt(vg_ref[...], pvo_ref[...])
    early[q, :, pl.ds(2 * r, r)] = dot_nt(hid_ref[...], pdi_ref[...])
    early[q, :, pl.ds(3 * r, r)] = dot_nt(x, pdo_ref[...])
    early[q, :, pl.ds(4 * r, 2 * r)] = jnp.broadcast_to(
        jnp.sum(xf * xf, axis=1, keepdims=True), (t, 2 * r)
    )
    early_copies = spread(early, early_sem, "query", q, Q)
    qpg = qpg_ref[...]
    md0 = jnp.sum(xf * gain * qpg.astype(F32), axis=1, keepdims=True) / D
    rg_out = dot_nt(rg_ref[...], pdo_ref[...])
    qpg_out = dot_nt(qpg, xs[pl.ds(B * t, r), :]) + dot_nt(qpg, xs[pl.ds(B * t + r, r), :])
    for copy in early_copies:
        copy.wait()
    whole = early[0]
    for i in range(1, Q):
        whole = whole + early[i]
    mask = mask_ref[...]
    inv = lax.rsqrt(whole[:, 4 * r :] / D + 1e-05)
    inv_col = inv[:, :1]
    inv_r = inv[:, :r]
    cubed = inv_r * inv_r * inv_r
    back = whole[:, 3 * r : 4 * r] * cubed
    hidden = whole[:, 2 * r : 3 * r] * mask[:, :r]
    pks[own, pl.ds(0, r)] = hidden
    pks[own, pl.ds(r, r)] = back
    pks[own, pl.ds(2 * r, 2 * r)] = inv
    for bi in range(1, B):
        copy = pltpu.make_async_remote_copy(
            src_ref=pks.at[own, :],
            dst_ref=pks.at[own, :],
            send_sem=pk_sem.at[0, bi],
            recv_sem=pk_sem.at[1, bi],
            device_id={"fsdp": a * B + lax.rem(b + bi, B)},
            device_id_type=MESH,
        )
        copy.start()
        waits.append(copy)
    normed = (xf * inv_col * gain).astype(BF16)
    attn = dot_nt(normed, pai_ref[...])
    kv_q[q, :, pl.ds(0, r)] = gram(whole[:, :r] * mask[:, :r], attn)
    kv_q[q, :, pl.ds(r, r)] = gram(whole[:, r : 2 * r] * mask[:, :r], attn)
    kv_copies = spread(kv_q, kv_q_sem, "query", q, Q)
    down0 = gram(rg_out + inv_r * qpg_out - back * md0, hidden)

    prod[...] = jnp.zeros_like(prod)
    proj[...] = jnp.zeros_like(proj)
    for copy in kv_copies:
        copy.wait()
    total = kv_q[0]
    for i in range(1, Q):
        total = total + kv_q[i]
    kv_f[f] = total
    kv_copies = spread(kv_f, kv_f_sem, "fsdp", f, F)
    for copy in waits:
        copy.wait()

    def block(weights, slot):
        y = jnp.dot(xs[...], weights, preferred_element_type=F32)
        cols = kgs[slot]
        prod[...] += y[: B * t] * cols.astype(F32)
        high, low = split(y[B * t : B * t + r] + y[B * t + r :])
        proj[...] += dot_nt(cols, high) + dot_nt(cols, low)

    block(w_ref[...], a)

    def step(s, carry):
        before, after = a - s, a + s

        @pl.when(before >= 0)
        def _():
            w_copy(w_ref, before, w_left, left).wait_recv()

        @pl.when((before >= 0) & has_right)
        def _():
            w_copy(wg.at[before], before, w_right, right).start()

        @pl.when(after < A)
        def _():
            w_copy(w_ref, after, w_right, right).wait_recv()

        @pl.when((after < A) & has_left)
        def _():
            w_copy(wg.at[after], after, w_left, left).start()

        @pl.when(before >= 0)
        def _():
            block(wg[before], before)

        @pl.when(after < A)
        def _():
            block(wg[after], after)

        return carry

    lax.fori_loop(1, A, step, 0)

    dots = jnp.sum(prod[...], axis=1, keepdims=True) / D
    packed = pks[...]
    late = packed[:, 2 * r : 3 * r] * proj[...] - packed[:, r : 2 * r] * dots
    d_q[q] = down0 + gram(late, packed[:, :r])
    for copy in spread(d_q, d_q_sem, "query", q, Q):
        copy.wait()
    total = d_q[0]
    for i in range(1, Q):
        total = total + d_q[i]
    d_f[f] = total
    d_copies = spread(d_f, d_f_sem, "fsdp", f, F)

    def drain(slot, carry):
        @pl.when((slot <= a) & has_right)
        def _():
            w_copy(w_ref, slot, w_right, right).wait_send()

        @pl.when((slot >= a) & has_left)
        def _():
            w_copy(w_ref, slot, w_left, left).wait_send()

        return carry

    lax.fori_loop(0, A, drain, 0)
    for copy in kv_copies:
        copy.wait()
    for buffer, out, copies in ((kv_f, out_kv, ()), (d_f, out_d, d_copies)):
        for copy in copies:
            copy.wait()
        for seq in range(seqs):
            total = buffer[seq * per_seq]
            for i in range(1, per_seq):
                total = total + buffer[seq * per_seq + i]
            out[seq] = total


def shards(
    F,
    Q,
    resid_in,
    resid_grad,
    query_path_grad,
    hidden_act,
    key_grad,
    value_grad,
    key_weight,
    value_weight,
    norm_gain,
    proj_attn_in,
    proj_key_out,
    proj_value_out,
    proj_down_in,
    proj_down_out,
    query_grads,
    seq_counts,
):
    B = 2
    A = F // B
    t, d = resid_in.shape
    w = key_weight.shape[1]
    r = proj_attn_in.shape[0]
    seqs = seq_counts.shape[0]
    n = key_grad.shape[1] // (w * B)
    fsdp_place = lax.axis_index("fsdp")

    def by_side(grad):
        return grad.reshape(t, n, B, w).transpose(2, 1, 0, 3)

    kgp = jnp.concatenate([by_side(key_grad), by_side(value_grad)], axis=3)
    weights = jnp.concatenate([key_weight, value_weight], axis=1)
    positions = fsdp_place * t + lax.iota(jnp.int32, t)
    limit = jnp.sum(
        jnp.where(
            (positions // LEN)[:, None] == lax.iota(jnp.int32, seqs)[None, :], seq_counts[None, :], 0
        ),
        axis=1,
    )
    mask = jnp.where(positions % LEN < limit, 1.0, 0.0).astype(F32)
    mask = jnp.broadcast_to(mask[:, None], (t, 2 * r))

    vmem = pl.BlockSpec(memory_space=pltpu.VMEM)
    dma = pltpu.SemaphoreType.DMA
    out_kv, out_d = pl.pallas_call(
        functools.partial(kernel, (F, Q, B, seqs)),
        out_shape=(
            jax.ShapeDtypeStruct((seqs, r, 2 * r), F32),
            jax.ShapeDtypeStruct((seqs, r, r), F32),
        ),
        in_specs=[vmem] * 15,
        out_specs=(vmem, vmem),
        scratch_shapes=[
            pltpu.VMEM((A, d, 2 * w), BF16),
            pltpu.VMEM((B * t + 2 * r, d), BF16),
            pltpu.VMEM((A, B * t, 2 * w), BF16),
            pltpu.VMEM((Q, t, 6 * r), F32),
            pltpu.VMEM((B * t, 4 * r), F32),
            pltpu.VMEM((B * t, 2 * w), F32),
            pltpu.VMEM((B * t, r), F32),
            pltpu.VMEM((Q, r, 2 * r), F32),
            pltpu.VMEM((F, r, 2 * r), F32),
            pltpu.VMEM((Q, r, r), F32),
            pltpu.VMEM((F, r, r), F32),
            dma((A,)),
            dma((A,)),
            dma((A,)),
            dma((2, B)),
            dma((B, Q)),
            dma((B, Q)),
            dma((2, Q)),
            dma((2, B)),
            dma((2, Q)),
            dma((2, F)),
            dma((2, Q)),
            dma((2, F)),
        ],
        compiler_params=pltpu.CompilerParams(
            collective_id=0, has_side_effects=True, vmem_limit_bytes=50 * 2**20
        ),
    )(
        resid_in,
        resid_grad,
        query_path_grad,
        hidden_act,
        key_grad,
        value_grad,
        kgp,
        weights,
        norm_gain.reshape(1, d),
        proj_attn_in,
        proj_key_out,
        proj_value_out,
        proj_down_in,
        proj_down_out,
        mask,
    )
    seq_grad = jnp.concatenate(
        [
            out_kv[:, :, :r].reshape(seqs, r * r),
            out_kv[:, :, r:].reshape(seqs, r * r),
            out_d.reshape(seqs, r * r),
        ],
        axis=1,
    )
    return jnp.dot(
        seq_grad,
        query_grads.astype(F32).T,
        precision=lax.Precision.HIGHEST,
        preferred_element_type=F32,
    )


def solution(mesh):
    placed = (
        P(("parts", "fsdp"), "query"),
        P(("parts", "fsdp"), "query"),
        P(("parts", "fsdp"), "query"),
        P(("parts", "fsdp"), "query"),
        P(("parts", "fsdp"), "query"),
        P(("parts", "fsdp"), "query"),
        P("query", "fsdp"),
        P("query", "fsdp"),
        P("query"),
        P(None, "query"),
        P(None, "query"),
        P(None, "query"),
        P(None, "query"),
        P(None, "query"),
        P(("fsdp", "query"), None),
        P("parts"),
    )
    return jax.shard_map(
        functools.partial(shards, mesh.shape["fsdp"], mesh.shape["query"]),
        mesh=mesh,
        in_specs=placed,
        out_specs=P("parts", ("fsdp", "query")),
        check_vma=False,
    )
```

time: 263 us -> 134 us (0.51)
  waiting for transfers between devices: 157 us -> 0 us
  Pallas kernels: 0 us -> 112 us
  blocking collectives: 60.5 us -> 0 us
  matrix products: 29.8 us -> 3.06 us
  local copies, waits for them, and re-layouts: 0.31 us -> 14.1 us
  between operations: 13.8 us -> 0.89 us
    all_gather x2 -> x0, waiting for transfers between devices: 125 us -> none  [the longest x1 70 us: shards(): lax.all_gather(value_weight, 'fsdp', axis=1, tiled=True)]
    pallas_call x0 -> x1, Pallas kernels: none -> 112 us  [shards(): pl.pallas_call(functools.partial(kernel, (F, Q, B, seqs)), out_shape=(jax...]
    psum x2 -> x0, blocking collectives: 43.7 us -> none  [the longest x1 37.5 us: shards(): seq_grad = lax.psum(local, 'fsdp')]
    psum x1 -> x0, waiting for transfers between devices: 30 us -> none  [shards(): lax.psum((jnp.sum(resid_f * resid_f, axis=1), early), 'query')]
    dot_general x11 -> x1, matrix products: 29.8 us -> 3.06 us  [shards(): jnp.dot(seq_grad, query_grads.astype(F32).T, precision=lax.Precision.HIGH...]
    all_gather x2 -> x0, blocking collectives: 16.8 us -> none  [the longest x1 9.07 us: shards(): lax.all_gather(key_grad, 'query', axis=1, tiled=True)]
    unnamed x10 -> x24, local copies, waits for them, and re-layouts: 0.05 us -> 7.98 us
    reshape x3 -> x6, local copies, waits for them, and re-layouts: 0.26 us -> 5.14 us  [the longest x2 3.31 us: by_side(): return grad.reshape(t, n, B, w).transpose(2, 1, 0, 3)]
  transfers between devices with their start and end apart: 3 -> 0, of which waited for: 3 -> 0; matrix products, arithmetic and copies ran while one was open for 5% -> 0% of each run, Pallas kernels for 0% -> 0%
where the time goes in v1:
time: 134 us
  Pallas kernels  112 us (84%)
  local copies, waits for them, and re-layouts  14.1 us (11%)
  other arithmetic  3.44 us (3%)
  matrix products  3.06 us (2%)
    pallas_call x1, Pallas kernels, shards(): pl.pallas_call(functools.partial(kernel, (F, Q, B, seqs)), out_shape=(jax...  112 us
    unnamed x24, local copies, waits for them, and re-layouts  7.98 us
    reshape x2, local copies, waits for them, and re-layouts, by_side(): return grad.reshape(t, n, B, w).transpose(2, 1, 0, 3)  3.31 us
    dot_general x1, matrix products, shards(): jnp.dot(seq_grad, query_grads.astype(F32).T, precision=lax.Precision.HIGH...  3.06 us

profile of v1, /device:TPU:0, one launch (start us, length us, event | category | flops | bytes accessed | tf_op | source)
XLA Modules:
  0.0 133.5 jit_solution(1099461782994893090)
XLA Ops:
  0.0 0.0 copy-start
  0.0 0.0 copy-start.4
  0.0 0.0 copy-start.3
  0.8 0.8 reshape.65.gain_ref
  1.6 0.1 broadcast_in_dim.32.mask_ref
  1.7 1.7 %copy.17 = bf16[256,256]{0,1:T(8,128)(2,1)} copy(bf16[256,256]{1,0:T(8,128)(2,1)} %kg_ref.1) | data formatting | bytes 262144 | tf_op args[4]
  3.4 1.7 %copy.18 = bf16[256,1,2,128]{3,0,1,2:T(8,128)(2,1)} copy(bf16[256,1,2,128]{0,3,2,1:T(8,128)(2,1)} %bitcast.12) | data formatting | bytes 262144 | tf_op jit(solution)/shard_map/reshape | solution.py:345
  5.1 1.7 %copy.19 = bf16[256,256]{0,1:T(8,128)(2,1)} copy(bf16[256,256]{1,0:T(8,128)(2,1)} %vg_ref.1) | data formatting | bytes 262144 | tf_op args[5]
  6.7 1.7 %copy.20 = bf16[256,1,2,128]{3,0,1,2:T(8,128)(2,1)} copy(bf16[256,1,2,128]{0,3,2,1:T(8,128)(2,1)} %bitcast.13) | data formatting | bytes 262144 | tf_op jit(solution)/shard_map/reshape | solution.py:345
  8.4 0.0 copy-start.1
  8.4 0.0 copy-start.2
  8.4 1.1 pad_maximum_fusion.1.kgp_ref
  9.5 2.3 %pad_maximum_fusion.w_ref = bf16[2048,256]{1,0:T(8,128)(2,1)} fusion(bf16[2048,128]{1,0:T(8,128)(2,1)} %param.23, bf16[2048,128]{1,0:T(8,128)(2,1)} %param.22), kind=kLoop, calls=%fused_computation | loop fusion | flops 2097152 | bytes 2097152 | tf_op jit(solution)/shard_map/concatenate | solution.py:348
  11.8 0.0 copy-done.4
  11.8 0.0 copy-done.3
  11.8 0.0 copy-done.1
  11.8 0.0 copy-done.2
  11.8 0.0 copy-start.5
  11.9 0.9 copy-done.5
  12.8 0.9 copy-done.6
  13.7 0.8 copy-done.8
  14.5 0.8 copy-done.9
  15.3 112.0 %shard_map.154 = (f32[1,64,128]{2,1,0:T(8,128)S(1)}, f32[1,64,64]{2,1,0:T(8,128)S(1)}) custom-call(bf16[256,2048]{1,0:T(8,128)(2,1)S(1)} %copy-done.1, bf16[256,2048]{1,0:T(8,128)(2,1)} %rg_ref.1, bf16[256,2048]{1,0:T(8,128)(2,1)} %qpg_ref.1, bf16[256,7168]{1,0:T(8,128)(2,1)} %hid_ref.1, bf16[256,256]{1,0:T(8,128)(2,1)S(1)} %copy-done.3, ...), custom_call_target="tpu_custom_call" | custom-call | tf_op jit(solution)/shard_map/pallas_call | solution.py:361
  127.3 0.0 copy-start.7
  127.3 0.6 copy-done.7
  127.9 0.6 copy-done.10
  128.5 0.8 reshape.68
  129.4 0.9 fusion.6
  130.3 0.1 reshape.66
  130.4 0.1 reshape.67
  130.5 0.0 copy-done
  130.5 3.1 %fusion = f32[1,128]{1,0:T(1,128)} fusion(bf16[128,12288]{1,0:T(8,128)(2,1)S(1)} %copy-done, f32[1,4096]{1,0:T(1,128)S(1)} %reshape.68, f32[1,4096]{1,0:T(1,128)S(1)} %reshape.67, f32[1,4096]{1,0:T(1,128)S(1)} %reshape.66), kind=kOutput, calls=%fused_computation.3 | convolution fusion | flops 18898944 | bytes 3195392 | tf_op jit(solution)/shard_map/dot_general | solution.py:422
  (5 shorter events, 0.0 us)
Async XLA Ops:
  0.0 130.5 %copy-start = (bf16[128,12288]{1,0:T(8,128)(2,1)S(1)}, bf16[128,12288]{1,0:T(8,128)(2,1)}, u32[]{:S(2)}) copy-start(bf16[128,12288]{1,0:T(8,128)(2,1)} %param.30) | copy-start | bytes 9437188
  0.0 11.8 %copy-start.4 = (bf16[256,256]{1,0:T(8,128)(2,1)S(1)}, bf16[256,256]{1,0:T(8,128)(2,1)}, u32[]{:S(2)}) copy-start(bf16[256,256]{1,0:T(8,128)(2,1)} %vg_ref.1) | copy-start | bytes 393220
  0.0 11.8 %copy-start.3 = (bf16[256,256]{1,0:T(8,128)(2,1)S(1)}, bf16[256,256]{1,0:T(8,128)(2,1)}, u32[]{:S(2)}) copy-start(bf16[256,256]{1,0:T(8,128)(2,1)} %kg_ref.1) | copy-start | bytes 393220
  8.4 3.4 %copy-start.1 = (bf16[256,2048]{1,0:T(8,128)(2,1)S(1)}, bf16[256,2048]{1,0:T(8,128)(2,1)}, u32[]{:S(2)}) copy-start(bf16[256,2048]{1,0:T(8,128)(2,1)} %x_ref.1) | copy-start | bytes 3145732
  8.4 3.4 %copy-start.2 = (bf16[64,7168]{1,0:T(8,128)(2,1)S(1)}, bf16[64,7168]{1,0:T(8,128)(2,1)}, u32[]{:S(2)}) copy-start(bf16[64,7168]{1,0:T(8,128)(2,1)} %pdi_ref.1) | copy-start | bytes 2752516
  11.8 1.0 copy-start.5
  12.8 0.9 copy-start.6
  13.7 0.8 copy-start.8
  14.5 0.8 copy-start.9
  127.3 0.6 copy-start.7
  127.9 0.6 copy-start.10

commit v2 on v1

v2 whole, which is shorter than its diff:
```python
import functools

import jax
import jax.numpy as jnp
from jax import lax
from jax.experimental import pallas as pl
from jax.experimental.pallas import tpu as pltpu
from jax.sharding import PartitionSpec as P

D = 8192
LEN = 2048
MESH = pl.DeviceIdType.MESH
F32 = jnp.float32
BF16 = jnp.bfloat16


def dot_nt(left, right):
    return lax.dot_general(left, right, (((1,), (1,)), ((), ())), preferred_element_type=F32)


def gram(left, right):
    return lax.dot_general(
        left,
        right,
        (((0,), (0,)), ((), ())),
        precision=lax.Precision.HIGHEST,
        preferred_element_type=F32,
    )


def split(value):
    high = value.astype(BF16)
    return high, (value - high.astype(F32)).astype(BF16)


def kernel(
    sizes,
    x_ref,
    rg_hbm,
    qpg_hbm,
    hid_hbm,
    kg_ref,
    vg_ref,
    wk_hbm,
    wv_hbm,
    gain_ref,
    pai_ref,
    pko_ref,
    pvo_ref,
    pdi_hbm,
    pdo_ref,
    grads_hbm,
    counts_ref,
    out_ref,
    rg_ref,
    qpg_ref,
    hid_ref,
    pdi_ref,
    grads_ref,
    wg,
    xs,
    kgp_ref,
    kgs,
    early,
    pks,
    prod,
    proj,
    kv_q,
    kv_f,
    d_q,
    d_f,
    flat,
    load_sem,
    w_recv,
    w_right,
    w_left,
    x_sem,
    kg_send,
    kg_recv,
    early_sem,
    pk_sem,
    kv_q_sem,
    kv_f_sem,
    d_q_sem,
    d_f_sem,
):
    F, Q, B, seqs = sizes
    A = F // B
    per_seq = F // seqs
    n = kgp_ref.shape[1]
    t, d = x_ref.shape
    w = wk_hbm.shape[1]
    r = pdo_ref.shape[0]
    f, q = lax.axis_index("fsdp"), lax.axis_index("query")
    a, b = f // B, lax.rem(f, B)

    barrier = pltpu.get_barrier_semaphore()
    others = 0
    for i in range(1, F):
        pl.semaphore_signal(
            barrier, inc=1, device_id={"fsdp": lax.rem(f + i, F)}, device_id_type=MESH
        )
        others += 1
    for bi in range(B):
        for qi in range(1, Q):
            pl.semaphore_signal(
                barrier,
                inc=1,
                device_id={"fsdp": a * B + lax.rem(b + bi, B), "query": lax.rem(q + qi, Q)},
                device_id_type=MESH,
            )
            others += 1

    loads = [
        pltpu.make_async_copy(src, dst, load_sem.at[i])
        for i, (src, dst) in enumerate(
            (
                (hid_hbm, hid_ref),
                (pdi_hbm, pdi_ref),
                (qpg_hbm, qpg_ref),
                (rg_hbm, rg_ref),
                (wk_hbm, wg.at[a, 0]),
                (wv_hbm, wg.at[a, 1]),
                (grads_hbm, grads_ref),
            )
        )
    ]
    for load in loads:
        load.start()
    gain = gain_ref[...].astype(F32)
    own = pl.ds(pl.multiple_of(b * t, t), t)
    xs[own, :] = (x_ref[...].astype(F32) * gain).astype(BF16)
    gp_high, gp_low = split(pdo_ref[...].astype(F32) * gain)
    xs[pl.ds(B * t, r), :] = gp_high
    xs[pl.ds(B * t + r, r), :] = gp_low
    for bi in range(B):
        for i in range(n):
            at = (i * B + bi) * w
            kgp_ref[bi, i, :, pl.ds(0, w)] = kg_ref[:, at : at + w]
            kgp_ref[bi, i, :, pl.ds(w, w)] = vg_ref[:, at : at + w]
    pl.semaphore_wait(barrier, others)

    right = {"fsdp": jnp.minimum(f + B, F - 1 - lax.rem(F - 1 - f, B))}
    left = {"fsdp": jnp.maximum(f - B, b)}
    has_right, has_left = a < A - 1, a > 0

    def w_copy(src, slot, part, send, target):
        return pltpu.make_async_remote_copy(
            src_ref=src,
            dst_ref=wg.at[slot, part],
            send_sem=send.at[slot, part],
            recv_sem=w_recv.at[slot, part],
            device_id=target,
            device_id_type=MESH,
        )

    for part, source in enumerate((wk_hbm, wv_hbm)):

        @pl.when(has_right)
        def _():
            w_copy(source, a, part, w_right, right).start()

        @pl.when(has_left)
        def _():
            w_copy(source, a, part, w_left, left).start()

    waits = []
    kgs[pl.ds(q * n, n), own, :] = kgp_ref[b]
    for bi in range(B):
        for qi in range(Q):
            if bi == 0 and qi == 0:
                continue
            there = lax.rem(b + bi, B)
            copy = pltpu.make_async_remote_copy(
                src_ref=kgp_ref.at[there],
                dst_ref=kgs.at[pl.ds(q * n, n), own, :],
                send_sem=kg_send.at[bi, qi],
                recv_sem=kg_recv.at[bi, qi],
                device_id={"fsdp": a * B + there, "query": lax.rem(q + qi, Q)},
                device_id_type=MESH,
            )
            copy.start()
            waits.append(copy)
    for bi in range(1, B):
        there = lax.rem(b + bi, B)
        copy = pltpu.make_async_remote_copy(
            src_ref=xs.at[own, :],
            dst_ref=xs.at[own, :],
            send_sem=x_sem.at[0, bi],
            recv_sem=x_sem.at[1, bi],
            device_id={"fsdp": a * B + there},
            device_id_type=MESH,
        )
        copy.start()
        waits.append(copy)

    def spread(buffer, sems, axis, me, count):
        copies = []
        for i in range(1, count):
            copy = pltpu.make_async_remote_copy(
                src_ref=buffer.at[me],
                dst_ref=buffer.at[me],
                send_sem=sems.at[0, i],
                recv_sem=sems.at[1, i],
                device_id={axis: lax.rem(me + i, count)},
                device_id_type=MESH,
            )
            copy.start()
            copies.append(copy)
        return copies

    def forward(s):
        before, after = a - s, a + s
        for part in range(2):

            @pl.when(before >= 0)
            def _():
                w_copy(wg.at[before, part], before, part, w_left, left).wait_recv()

            @pl.when((before >= 0) & has_right)
            def _():
                w_copy(wg.at[before, part], before, part, w_right, right).start()

            @pl.when(after < A)
            def _():
                w_copy(wg.at[after, part], after, part, w_right, right).wait_recv()

            @pl.when((after < A) & has_left)
            def _():
                w_copy(wg.at[after, part], after, part, w_left, left).start()

    def block(slot):
        weights = jnp.concatenate([wg[slot, 0], wg[slot, 1]], axis=1)
        y = jnp.dot(xs[...], weights, preferred_element_type=F32)
        cols = kgs[slot]
        prod[...] += y[: B * t] * cols.astype(F32)
        high, low = split(y[B * t : B * t + r] + y[B * t + r :])
        proj[...] += dot_nt(cols, high) + dot_nt(cols, low)

    def contract(s):
        @pl.when(a - s >= 0)
        def _():
            block(a - s)

        @pl.when(a + s < A)
        def _():
            block(a + s)

    x = x_ref[...]
    xf = x.astype(F32)
    early[q, :, pl.ds(0, r)] = dot_nt(kg_ref[...], pko_ref[...])
    early[q, :, pl.ds(r, r)] = dot_nt(vg_ref[...], pvo_ref[...])
    early[q, :, pl.ds(3 * r, r)] = dot_nt(x, pdo_ref[...])
    early[q, :, pl.ds(4 * r, 2 * r)] = jnp.broadcast_to(
        jnp.sum(xf * xf, axis=1, keepdims=True), (t, 2 * r)
    )
    for load in loads:
        load.wait()
    early[q, :, pl.ds(2 * r, r)] = dot_nt(hid_ref[...], pdi_ref[...])
    early_copies = spread(early, early_sem, "query", q, Q)
    qpg = qpg_ref[...]
    md0 = jnp.sum(xf * gain * qpg.astype(F32), axis=1, keepdims=True) / D
    rg_out = dot_nt(rg_ref[...], pdo_ref[...])
    qpg_out = dot_nt(qpg, xs[pl.ds(B * t, r), :]) + dot_nt(qpg, xs[pl.ds(B * t + r, r), :])
    prod[...] = jnp.zeros_like(prod)
    proj[...] = jnp.zeros_like(proj)

    forward(1)
    for copy in early_copies:
        copy.wait()
    whole = early[0]
    for i in range(1, Q):
        whole = whole + early[i]
    place = f // per_seq
    limit = jnp.int32(0)
    for seq in range(seqs):
        limit += jnp.where(place == seq, counts_ref[seq], 0)
    position = lax.rem(f, per_seq) * t + lax.broadcasted_iota(jnp.int32, (t, r), 0)
    mask = jnp.where(position < limit, 1.0, 0.0).astype(F32)
    inv = lax.rsqrt(whole[:, 4 * r :] / D + 1e-05)
    inv_col = inv[:, :1]
    inv_r = inv[:, :r]
    cubed = inv_r * inv_r * inv_r
    back = whole[:, 3 * r : 4 * r] * cubed
    hidden = whole[:, 2 * r : 3 * r] * mask
    pks[own, pl.ds(0, r)] = hidden
    pks[own, pl.ds(r, r)] = back
    pks[own, pl.ds(2 * r, 2 * r)] = inv
    for bi in range(1, B):
        copy = pltpu.make_async_remote_copy(
            src_ref=pks.at[own, :],
            dst_ref=pks.at[own, :],
            send_sem=pk_sem.at[0, bi],
            recv_sem=pk_sem.at[1, bi],
            device_id={"fsdp": a * B + lax.rem(b + bi, B)},
            device_id_type=MESH,
        )
        copy.start()
        waits.append(copy)
    normed = (xf * inv_col * gain).astype(BF16)
    attn = dot_nt(normed, pai_ref[...])
    kv_q[q, :, pl.ds(0, r)] = gram(whole[:, :r] * mask, attn)
    kv_q[q, :, pl.ds(r, r)] = gram(whole[:, r : 2 * r] * mask, attn)
    kv_copies = spread(kv_q, kv_q_sem, "query", q, Q)
    down0 = gram(rg_out + inv_r * qpg_out - back * md0, hidden)

    if A > 2:
        forward(2)
    for copy in waits:
        copy.wait()
    for copy in kv_copies:
        copy.wait()
    total = kv_q[0]
    for i in range(1, Q):
        total = total + kv_q[i]
    kv_f[f] = total
    kv_copies = spread(kv_f, kv_f_sem, "fsdp", f, F)
    block(a)
    contract(1)

    def step(s, carry):
        forward(s)
        contract(s - 1)
        return carry

    def by_query(total, at):
        for seq in range(seqs):
            for i in range(r):
                flat[seq, pl.ds(0, 1), pl.ds(at + i * r, r)] = total[seq][i : i + 1, :]

    def score(start, size):
        grads = grads_ref[:, start : start + size]
        parts = []
        for seq in range(seqs):
            row = jnp.broadcast_to(flat[seq, pl.ds(0, 1), pl.ds(start, size)], (16, size))
            high = row.astype(BF16)
            rest = row - high.astype(F32)
            middle = rest.astype(BF16)
            low = (rest - middle.astype(F32)).astype(BF16)
            value = dot_nt(high, grads) + (dot_nt(middle, grads) + dot_nt(low, grads))
            parts.append(value[:1])
        return parts

    def sequences(buffer):
        totals = []
        for seq in range(seqs):
            total = buffer[seq * per_seq]
            for i in range(1, per_seq):
                total = total + buffer[seq * per_seq + i]
            totals.append(total)
        return totals

    if A > 2:
        lax.fori_loop(3, A, step, 0)
    for copy in kv_copies:
        copy.wait()
    totals = sequences(kv_f)
    by_query([total[:, :r] for total in totals], 0)
    by_query([total[:, r:] for total in totals], r * r)
    scores = score(0, 2 * r * r)
    if A > 2:
        contract(A - 1)

    dots = jnp.sum(prod[...], axis=1, keepdims=True) / D
    packed = pks[...]
    late = packed[:, 2 * r : 3 * r] * proj[...] - packed[:, r : 2 * r] * dots
    d_q[q] = down0 + gram(late, packed[:, :r])
    for copy in spread(d_q, d_q_sem, "query", q, Q):
        copy.wait()
    total = d_q[0]
    for i in range(1, Q):
        total = total + d_q[i]
    d_f[f] = total
    d_copies = spread(d_f, d_f_sem, "fsdp", f, F)

    def drain(slot, carry):
        for part in range(2):

            @pl.when((slot <= a) & has_right)
            def _():
                w_copy(wg.at[slot, part], slot, part, w_right, right).wait_send()

            @pl.when((slot >= a) & has_left)
            def _():
                w_copy(wg.at[slot, part], slot, part, w_left, left).wait_send()

        return carry

    lax.fori_loop(0, A, drain, 0)
    for copy in d_copies:
        copy.wait()
    by_query(sequences(d_f), 2 * r * r)
    for seq, late_scores in enumerate(score(2 * r * r, r * r)):
        out_ref[pl.ds(seq, 1), :] = scores[seq] + late_scores


def shards(
    F,
    Q,
    resid_in,
    resid_grad,
    query_path_grad,
    hidden_act,
    key_grad,
    value_grad,
    key_weight,
    value_weight,
    norm_gain,
    proj_attn_in,
    proj_key_out,
    proj_value_out,
    proj_down_in,
    proj_down_out,
    query_grads,
    seq_counts,
):
    B = 2
    A = F // B
    t, d = resid_in.shape
    w = key_weight.shape[1]
    r = proj_attn_in.shape[0]
    seqs = seq_counts.shape[0]
    n = key_grad.shape[1] // (w * B)
    vmem = pl.BlockSpec(memory_space=pltpu.VMEM)
    hbm = pl.BlockSpec(memory_space=pl.ANY)
    dma = pltpu.SemaphoreType.DMA
    operands = (
        (resid_in, vmem),
        (resid_grad, hbm),
        (query_path_grad, hbm),
        (hidden_act, hbm),
        (key_grad, vmem),
        (value_grad, vmem),
        (key_weight, hbm),
        (value_weight, hbm),
        (norm_gain.reshape(1, d), vmem),
        (proj_attn_in, vmem),
        (proj_key_out, vmem),
        (proj_value_out, vmem),
        (proj_down_in, hbm),
        (proj_down_out, vmem),
        (query_grads, hbm),
        (seq_counts, pl.BlockSpec(memory_space=pltpu.SMEM)),
    )
    return pl.pallas_call(
        functools.partial(kernel, (F, Q, B, seqs)),
        out_shape=jax.ShapeDtypeStruct((seqs, query_grads.shape[0]), F32),
        in_specs=[spec for _, spec in operands],
        out_specs=vmem,
        scratch_shapes=[
            pltpu.VMEM(resid_grad.shape, BF16),
            pltpu.VMEM(query_path_grad.shape, BF16),
            pltpu.VMEM(hidden_act.shape, BF16),
            pltpu.VMEM(proj_down_in.shape, BF16),
            pltpu.VMEM(query_grads.shape, BF16),
            pltpu.VMEM((A, 2, d, w), BF16),
            pltpu.VMEM((B * t + 2 * r, d), BF16),
            pltpu.VMEM((B, n, t, 2 * w), BF16),
            pltpu.VMEM((A, B * t, 2 * w), BF16),
            pltpu.VMEM((Q, t, 6 * r), F32),
            pltpu.VMEM((B * t, 4 * r), F32),
            pltpu.VMEM((B * t, 2 * w), F32),
            pltpu.VMEM((B * t, r), F32),
            pltpu.VMEM((Q, r, 2 * r), F32),
            pltpu.VMEM((F, r, 2 * r), F32),
            pltpu.VMEM((Q, r, r), F32),
            pltpu.VMEM((F, r, r), F32),
            pltpu.VMEM((seqs, 8, 3 * r * r), F32),
            dma((7,)),
            dma((A, 2)),
            dma((A, 2)),
            dma((A, 2)),
            dma((2, B)),
            dma((B, Q)),
            dma((B, Q)),
            dma((2, Q)),
            dma((2, B)),
            dma((2, Q)),
            dma((2, F)),
            dma((2, Q)),
            dma((2, F)),
        ],
        compiler_params=pltpu.CompilerParams(
            collective_id=0, has_side_effects=True, vmem_limit_bytes=56 * 2**20
        ),
    )(*(operand for operand, _ in operands))


def solution(mesh):
    placed = (
        P(("parts", "fsdp"), "query"),
        P(("parts", "fsdp"), "query"),
        P(("parts", "fsdp"), "query"),
        P(("parts", "fsdp"), "query"),
        P(("parts", "fsdp"), "query"),
        P(("parts", "fsdp"), "query"),
        P("query", "fsdp"),
        P("query", "fsdp"),
        P("query"),
        P(None, "query"),
        P(None, "query"),
        P(None, "query"),
        P(None, "query"),
        P(None, "query"),
        P(("fsdp", "query"), None),
        P("parts"),
    )
    return jax.shard_map(
        functools.partial(shards, mesh.shape["fsdp"], mesh.shape["query"]),
        mesh=mesh,
        in_specs=placed,
        out_specs=P("parts", ("fsdp", "query")),
        check_vma=False,
    )
```

time: 134 us -> 99.2 us (0.74)
  Pallas kernels: 112 us -> 95.9 us
  local copies, waits for them, and re-layouts: 14.1 us -> 2.4 us
  other arithmetic: 3.44 us -> 0 us
  matrix products: 3.06 us -> 0 us
    pallas_call x1, Pallas kernels: 112 us -> 95.9 us  [shards(): pl.pallas_call(functools.partial(kernel, (F, Q, B, seqs)), out_shape=jax....]
    unnamed x24 -> x1, local copies, waits for them, and re-layouts: 7.98 us -> 1.11 us
    reshape x5 -> x0, local copies, waits for them, and re-layouts: 4.33 us -> none  [the longest x2 3.31 us: by_side(): return grad.reshape(t, n, B, w).transpose(2, 1, 0, 3)]
    concatenate x2 -> x0, other arithmetic: 3.43 us -> none  [the longest x1 2.29 us: shards(): weights = jnp.concatenate([key_weight, value_weight], axis=1)]
    dot_general x1 -> x0, matrix products: 3.06 us -> none  [shards(): jnp.dot(seq_grad, query_grads.astype(F32).T, precision=lax.Precision.HIGH...]
where the time goes in v2:
time: 99.2 us; the launch traced here: 99 us
  Pallas kernels  95.9 us (97%)
  local copies, waits for them, and re-layouts  2.4 us (2%)
    pallas_call x1, Pallas kernels, shards(): pl.pallas_call(functools.partial(kernel, (F, Q, B, seqs)), out_shape=jax....  95.9 us

profile of v2, /device:TPU:0, one launch (start us, length us, event | category | flops | bytes accessed | tf_op | source)
XLA Modules:
  0.0 99.0 jit_solution(7766007591841328838)
XLA Ops:
  0.7 1.3 %reshape.3.gain_ref = bf16[1,2048]{1,0:T(2,128)(2,1)} reshape(bf16[2048]{0:T(1024)(128)(2,1)} %param.24) | data formatting | bytes 8192 | tf_op jit(solution)/shard_map/reshape | solution.py:436
  1.9 95.9 %shard_map.154 = f32[1,128]{1,0:T(1,128)} custom-call(bf16[256,2048]{1,0:T(8,128)(2,1)} %x_ref.1, bf16[256,2048]{1,0:T(8,128)(2,1)} %rg_hbm.1, bf16[256,2048]{1,0:T(8,128)(2,1)} %qpg_hbm.1, bf16[256,7168]{1,0:T(8,128)(2,1)} %hid_hbm.1, bf16[256,256]{1,0:T(8,128)(2,1)} %kg_ref.1, bf16[256,256]{1,0:T(8,128)(2,1)} %vg_ref.1, bf16[2048,128]{1,0:T(8,128)(2,1)} %wk_hbm.1, ...), custom_call_target="tpu_custom_call" | custom-call | tf_op jit(solution)/shard_map/pallas_call | solution.py:445
  97.9 1.1 %copy.19 = f32[1,128]{1,0:T(1,128)} copy(f32[1,128]{1,0:T(1,128)} %shard_map.154) | data formatting | bytes 1024

commit v3 on v2

--- a/solution.py
+++ b/solution.py
@@ -9,6 +9,7 @@
 
 D = 8192
 LEN = 2048
+CHUNKS = 4
 MESH = pl.DeviceIdType.MESH
 F32 = jnp.float32
 BF16 = jnp.bfloat16
@@ -75,10 +76,16 @@
     w_right,
     w_left,
     x_sem,
-    kg_send,
-    kg_recv,
+    x_end_sem,
+    x_extra_sem,
+    kg_pair_sem,
+    kg_sem,
+    kg_end_sem,
+    kg_extra_sem,
     early_sem,
     pk_sem,
+    pk_end_sem,
+    pk_extra_sem,
     kv_q_sem,
     kv_f_sem,
     d_q_sem,
@@ -101,15 +108,11 @@
             barrier, inc=1, device_id={"fsdp": lax.rem(f + i, F)}, device_id_type=MESH
         )
         others += 1
-    for bi in range(B):
-        for qi in range(1, Q):
-            pl.semaphore_signal(
-                barrier,
-                inc=1,
-                device_id={"fsdp": a * B + lax.rem(b + bi, B), "query": lax.rem(q + qi, Q)},
-                device_id_type=MESH,
-            )
-            others += 1
+    for qi in range(1, Q):
+        pl.semaphore_signal(
+            barrier, inc=1, device_id={"query": lax.rem(q + qi, Q)}, device_id_type=MESH
+        )
+        others += 1
 
     loads = [
         pltpu.make_async_copy(src, dst, load_sem.at[i])
@@ -142,7 +145,64 @@
 
     right = {"fsdp": jnp.minimum(f + B, F - 1 - lax.rem(F - 1 - f, B))}
     left = {"fsdp": jnp.maximum(f - B, b)}
-    has_right, has_left = a < A - 1, a > 0
+    is_end = (a == 0) | (a == A - 1)
+    is_host = (a > 0) & (a < A - 1)
+    has_extra = (a == 1) | (a == A - 2)
+    inward = {"fsdp": jnp.where(a == 0, f + B, f - B)}
+    has_right, has_left = a < A - 2, a > 1
+    extra = B * t + 2 * r
+    piece = t // CHUNKS
+
+    def remote(src, dst, sems, at, target):
+        return pltpu.make_async_remote_copy(
+            src_ref=src,
+            dst_ref=dst,
+            send_sem=sems.at[(0,) + at],
+            recv_sem=sems.at[(1,) + at],
+            device_id=target,
+            device_id_type=MESH,
+        )
+
+    def start(copies):
+        for copy in copies:
+            copy.start()
+
+    def finish(copies):
+        for copy in copies:
+            copy.wait()
+
+    partners = [{"fsdp": a * B + lax.rem(b + bi, B)} for bi in range(1, B)]
+    peers = [{"query": lax.rem(q + qi, Q)} for qi in range(1, Q)]
+    mine = pl.ds(q * n, n)
+
+    def paired(ref, sems, at=()):
+        return [remote(ref, ref, sems, at + (bi + 1,), there) for bi, there in enumerate(partners)]
+
+    def x_rows(first, i):
+        return xs.at[pl.ds(pl.multiple_of(first + b * t + i * piece, 16), piece), :]
+
+    x_pair = paired(xs.at[own, :], x_sem)
+    kg_pair = [
+        remote(
+            kgp_ref.at[lax.rem(b + bi, B)], kgs.at[0, mine, own, :], kg_pair_sem, (bi,), partners[bi - 1]
+        )
+        for bi in range(1, B)
+    ]
+    kg_peers, kg_extra = (
+        [
+            remote(kgs.at[g, mine], kgs.at[g, mine], sems, (qi + 1,), there)
+            for qi, there in enumerate(peers)
+        ]
+        for g, sems in ((0, kg_sem), (1, kg_extra_sem))
+    )
+    kg_end = remote(kgs.at[0, mine], kgs.at[1, mine], kg_end_sem, (), inward)
+    x_end = [
+        remote(x_rows(0, i), x_rows(extra, i), x_end_sem, (i,), inward) for i in range(CHUNKS)
+    ]
+    x_extra = [paired(x_rows(extra, i), x_extra_sem, (i,)) for i in range(CHUNKS)]
+    pk_pair = paired(pks.at[0, own, :], pk_sem)
+    pk_end = remote(pks.at[0, own, :], pks.at[1, own, :], pk_end_sem, (), inward)
+    pk_extra = paired(pks.at[1, own, :], pk_extra_sem)
 
     def w_copy(src, slot, part, send, target):
         return pltpu.make_async_remote_copy(
@@ -164,35 +224,12 @@
         def _():
             w_copy(source, a, part, w_left, left).start()
 
-    waits = []
-    kgs[pl.ds(q * n, n), own, :] = kgp_ref[b]
-    for bi in range(B):
-        for qi in range(Q):
-            if bi == 0 and qi == 0:
-                continue
-            there = lax.rem(b + bi, B)
-            copy = pltpu.make_async_remote_copy(
-                src_ref=kgp_ref.at[there],
-                dst_ref=kgs.at[pl.ds(q * n, n), own, :],
-                send_sem=kg_send.at[bi, qi],
-                recv_sem=kg_recv.at[bi, qi],
-                device_id={"fsdp": a * B + there, "query": lax.rem(q + qi, Q)},
-                device_id_type=MESH,
-            )
-            copy.start()
-            waits.append(copy)
-    for bi in range(1, B):
-        there = lax.rem(b + bi, B)
-        copy = pltpu.make_async_remote_copy(
-            src_ref=xs.at[own, :],
-            dst_ref=xs.at[own, :],
-            send_sem=x_sem.at[0, bi],
-            recv_sem=x_sem.at[1, bi],
-            device_id={"fsdp": a * B + there},
-            device_id_type=MESH,
-        )
-        copy.start()
-        waits.append(copy)
+    kgs[0, mine, own, :] = kgp_ref[b]
+    start(kg_pair)
+
+    @pl.when(is_host)
+    def _():
+        start(x_pair)
 
     def spread(buffer, sems, axis, me, count):
         copies = []
@@ -213,38 +250,60 @@
         before, after = a - s, a + s
         for part in range(2):
 
-            @pl.when(before >= 0)
+            @pl.when(is_host & (before >= 0))
             def _():
                 w_copy(wg.at[before, part], before, part, w_left, left).wait_recv()
 
-            @pl.when((before >= 0) & has_right)
+            @pl.when(is_host & (before >= 0) & has_right)
             def _():
                 w_copy(wg.at[before, part], before, part, w_right, right).start()
 
-            @pl.when(after < A)
+            @pl.when(is_host & (after < A))
             def _():
                 w_copy(wg.at[after, part], after, part, w_right, right).wait_recv()
 
-            @pl.when((after < A) & has_left)
+            @pl.when(is_host & (after < A) & has_left)
             def _():
                 w_copy(wg.at[after, part], after, part, w_left, left).start()
 
     def block(slot):
         weights = jnp.concatenate([wg[slot, 0], wg[slot, 1]], axis=1)
-        y = jnp.dot(xs[...], weights, preferred_element_type=F32)
-        cols = kgs[slot]
-        prod[...] += y[: B * t] * cols.astype(F32)
+        y = jnp.dot(xs[pl.ds(0, extra), :], weights, preferred_element_type=F32)
         high, low = split(y[B * t : B * t + r] + y[B * t + r :])
-        proj[...] += dot_nt(cols, high) + dot_nt(cols, low)
+
+        def add(g, value):
+            cols = kgs[g, slot]
+            prod[g] += value * cols.astype(F32)
+            proj[g] += dot_nt(cols, high) + dot_nt(cols, low)
+
+        add(0, y[: B * t])
+
+        @pl.when(has_extra)
+        def _():
+            add(1, jnp.dot(xs[pl.ds(extra, B * t), :], weights, preferred_element_type=F32))
 
     def contract(s):
-        @pl.when(a - s >= 0)
+        @pl.when(is_host & (a - s >= 0))
         def _():
             block(a - s)
 
-        @pl.when(a + s < A)
+        @pl.when(is_host & (a + s < A))
         def _():
             block(a + s)
+
+    def pass_rows(first, last):
+        for i in range(first, last):
+
+            @pl.when(has_extra)
+            def _():
+                x_end[i].wait_recv()
+                start(x_extra[i])
+
+            @pl.when(is_end)
+            def _():
+                if i + 1 < CHUNKS:
+                    x_end[i].wait_send()
+                    x_end[i + 1].start()
 
     x = x_ref[...]
     xf = x.astype(F32)
@@ -265,9 +324,30 @@
     prod[...] = jnp.zeros_like(prod)
     proj[...] = jnp.zeros_like(proj)
 
+    finish(kg_pair)
+
+    @pl.when(is_host)
+    def _():
+        start(kg_peers)
+
     forward(1)
-    for copy in early_copies:
-        copy.wait()
+
+    @pl.when(is_end)
+    def _():
+        for part in range(2):
+
+            @pl.when(has_right)
+            def _():
+                w_copy(wg.at[a, part], a, part, w_right, right).wait_send()
+
+            @pl.when(has_left)
+            def _():
+                w_copy(wg.at[a, part], a, part, w_left, left).wait_send()
+
+        x_end[0].start()
+        kg_end.start()
+
+    finish(early_copies)
     whole = early[0]
     for i in range(1, Q):
         whole = whole + early[i]
@@ -283,31 +363,32 @@
     cubed = inv_r * inv_r * inv_r
     back = whole[:, 3 * r : 4 * r] * cubed
     hidden = whole[:, 2 * r : 3 * r] * mask
-    pks[own, pl.ds(0, r)] = hidden
-    pks[own, pl.ds(r, r)] = back
-    pks[own, pl.ds(2 * r, 2 * r)] = inv
-    for bi in range(1, B):
-        copy = pltpu.make_async_remote_copy(
-            src_ref=pks.at[own, :],
-            dst_ref=pks.at[own, :],
-            send_sem=pk_sem.at[0, bi],
-            recv_sem=pk_sem.at[1, bi],
-            device_id={"fsdp": a * B + lax.rem(b + bi, B)},
-            device_id_type=MESH,
-        )
-        copy.start()
-        waits.append(copy)
+    pks[0, own, pl.ds(0, r)] = hidden * inv_r
+    pks[0, own, pl.ds(r, r)] = whole[:, 3 * r : 4 * r] * (inv_r * inv_r)
+
+    @pl.when(is_host)
+    def _():
+        start(pk_pair)
+
+    @pl.when(is_end)
+    def _():
+        pk_end.start()
+
+    @pl.when(has_extra)
+    def _():
+        kg_end.wait_recv()
+        start(kg_extra)
+
+    pass_rows(0, 1)
     normed = (xf * inv_col * gain).astype(BF16)
     attn = dot_nt(normed, pai_ref[...])
     kv_q[q, :, pl.ds(0, r)] = gram(whole[:, :r] * mask, attn)
     kv_q[q, :, pl.ds(r, r)] = gram(whole[:, r : 2 * r] * mask, attn)
     kv_copies = spread(kv_q, kv_q_sem, "query", q, Q)
+    pass_rows(1, 2)
     down0 = gram(rg_out + inv_r * qpg_out - back * md0, hidden)
 
-    if A > 2:
-        forward(2)
-    for copy in waits:
-        copy.wait()
+    pass_rows(2, 3)
     for copy in kv_copies:
         copy.wait()
     total = kv_q[0]
@@ -315,7 +396,38 @@
         total = total + kv_q[i]
     kv_f[f] = total
     kv_copies = spread(kv_f, kv_f_sem, "fsdp", f, F)
-    block(a)
+    pass_rows(3, CHUNKS)
+
+    @pl.when(has_extra)
+    def _():
+        pk_end.wait_recv()
+        start(pk_extra)
+
+    forward(2)
+
+    @pl.when(is_end)
+    def _():
+        x_end[CHUNKS - 1].wait_send()
+        kg_end.wait_send()
+        pk_end.wait_send()
+
+    @pl.when(is_host)
+    def _():
+        finish(x_pair)
+        finish(kg_peers)
+        finish(pk_pair)
+
+    @pl.when(has_extra)
+    def _():
+        finish(kg_extra)
+        for copies in x_extra:
+            finish(copies)
+        finish(pk_extra)
+
+    @pl.when(is_host)
+    def _():
+        block(a)
+
     contract(1)
 
     def step(s, carry):
@@ -350,21 +462,29 @@
             totals.append(total)
         return totals
 
-    if A > 2:
-        lax.fori_loop(3, A, step, 0)
+    lax.fori_loop(3, A - 1, step, 0)
     for copy in kv_copies:
         copy.wait()
     totals = sequences(kv_f)
     by_query([total[:, :r] for total in totals], 0)
     by_query([total[:, r:] for total in totals], r * r)
     scores = score(0, 2 * r * r)
-    if A > 2:
-        contract(A - 1)
-
-    dots = jnp.sum(prod[...], axis=1, keepdims=True) / D
-    packed = pks[...]
-    late = packed[:, 2 * r : 3 * r] * proj[...] - packed[:, r : 2 * r] * dots
-    d_q[q] = down0 + gram(late, packed[:, :r])
+    contract(A - 2)
+
+    d_q[q] = down0
+
+    def add_gram(g):
+        dots = jnp.sum(prod[g], axis=1, keepdims=True) / D
+        d_q[q] += gram(proj[g] - pks[g, :, pl.ds(r, r)] * dots, pks[g, :, pl.ds(0, r)])
+
+    @pl.when(is_host)
+    def _():
+        add_gram(0)
+
+    @pl.when(has_extra)
+    def _():
+        add_gram(1)
+
     for copy in spread(d_q, d_q_sem, "query", q, Q):
         copy.wait()
     total = d_q[0]
@@ -376,11 +496,11 @@
     def drain(slot, carry):
         for part in range(2):
 
-            @pl.when((slot <= a) & has_right)
+            @pl.when((slot <= a) & has_right & is_host)
             def _():
                 w_copy(wg.at[slot, part], slot, part, w_right, right).wait_send()
 
-            @pl.when((slot >= a) & has_left)
+            @pl.when((slot >= a) & has_left & is_host)
             def _():
                 w_copy(wg.at[slot, part], slot, part, w_left, left).wait_send()
 
@@ -454,13 +574,13 @@
             pltpu.VMEM(proj_down_in.shape, BF16),
             pltpu.VMEM(query_grads.shape, BF16),
             pltpu.VMEM((A, 2, d, w), BF16),
-            pltpu.VMEM((B * t + 2 * r, d), BF16),
+            pltpu.VMEM((2 * B * t + 2 * r, d), BF16),
             pltpu.VMEM((B, n, t, 2 * w), BF16),
-            pltpu.VMEM((A, B * t, 2 * w), BF16),
+            pltpu.VMEM((2, A, B * t, 2 * w), BF16),
             pltpu.VMEM((Q, t, 6 * r), F32),
-            pltpu.VMEM((B * t, 4 * r), F32),
-            pltpu.VMEM((B * t, 2 * w), F32),
-            pltpu.VMEM((B * t, r), F32),
+            pltpu.VMEM((2, B * t, 2 * r), F32),
+            pltpu.VMEM((2, B * t, 2 * w), F32),
+            pltpu.VMEM((2, B * t, r), F32),
             pltpu.VMEM((Q, r, 2 * r), F32),
             pltpu.VMEM((F, r, 2 * r), F32),
             pltpu.VMEM((Q, r, r), F32),
@@ -471,9 +591,15 @@
             dma((A, 2)),
             dma((A, 2)),
             dma((2, B)),
-            dma((B, Q)),
-            dma((B, Q)),
+            dma((2, CHUNKS)),
+            dma((2, CHUNKS, B)),
+            dma((2, B)),
             dma((2, Q)),
+            dma((2,)),
+            dma((2, Q)),
+            dma((2, Q)),
+            dma((2, B)),
+            dma((2,)),
             dma((2, B)),
             dma((2, Q)),
             dma((2, F)),

time: 99.2 us -> 100 us (level)
  Pallas kernels: 95.9 us -> 97.1 us
    pallas_call x1, Pallas kernels: 95.9 us -> 97.1 us  [shards(): pl.pallas_call(functools.partial(kernel, (F, Q, B, seqs)), out_shape=jax....]
where the time goes in v3:
time: 100 us
  Pallas kernels  97.1 us (97%)
  local copies, waits for them, and re-layouts  2.4 us (2%)
    pallas_call x1, Pallas kernels, shards(): pl.pallas_call(functools.partial(kernel, (F, Q, B, seqs)), out_shape=jax....  97.1 us

profile of v3, /device:TPU:0, one launch (start us, length us, event | category | flops | bytes accessed | tf_op | source)
XLA Modules:
  0.0 100.1 jit_solution(1208414923571553835)
XLA Ops:
  0.7 1.3 %reshape.3.gain_ref = bf16[1,2048]{1,0:T(2,128)(2,1)} reshape(bf16[2048]{0:T(1024)(128)(2,1)} %param.24) | data formatting | bytes 8192 | tf_op jit(solution)/shard_map/reshape | solution.py:556
  1.9 97.1 %shard_map.154 = f32[1,128]{1,0:T(1,128)} custom-call(bf16[256,2048]{1,0:T(8,128)(2,1)} %x_ref.1, bf16[256,2048]{1,0:T(8,128)(2,1)} %rg_hbm.1, bf16[256,2048]{1,0:T(8,128)(2,1)} %qpg_hbm.1, bf16[256,7168]{1,0:T(8,128)(2,1)} %hid_hbm.1, bf16[256,256]{1,0:T(8,128)(2,1)} %kg_ref.1, bf16[256,256]{1,0:T(8,128)(2,1)} %vg_ref.1, bf16[2048,128]{1,0:T(8,128)(2,1)} %wk_hbm.1, ...), custom_call_target="tpu_custom_call" | custom-call | tf_op jit(solution)/shard_map/pallas_call | solution.py:565
  99.0 1.1 %copy.19 = f32[1,128]{1,0:T(1,128)} copy(f32[1,128]{1,0:T(1,128)} %shard_map.154) | data formatting | bytes 1024

commit v4 on v3

--- a/solution.py
+++ b/solution.py
@@ -63,6 +63,7 @@
     kgp_ref,
     kgs,
     early,
+    squares,
     pks,
     prod,
     proj,
@@ -83,6 +84,7 @@
     kg_end_sem,
     kg_extra_sem,
     early_sem,
+    squares_sem,
     pk_sem,
     pk_end_sem,
     pk_extra_sem,
@@ -266,57 +268,44 @@
             def _():
                 w_copy(wg.at[after, part], after, part, w_left, left).start()
 
-    def block(slot):
+    def block(g, slot):
         weights = jnp.concatenate([wg[slot, 0], wg[slot, 1]], axis=1)
-        y = jnp.dot(xs[pl.ds(0, extra), :], weights, preferred_element_type=F32)
-        high, low = split(y[B * t : B * t + r] + y[B * t + r :])
-
-        def add(g, value):
-            cols = kgs[g, slot]
-            prod[g] += value * cols.astype(F32)
-            proj[g] += dot_nt(cols, high) + dot_nt(cols, low)
-
-        add(0, y[: B * t])
-
-        @pl.when(has_extra)
-        def _():
-            add(1, jnp.dot(xs[pl.ds(extra, B * t), :], weights, preferred_element_type=F32))
+        rows = xs[pl.ds(g * B * t, extra), :]
+        y = jnp.dot(rows, weights, preferred_element_type=F32)
+        gains = y[B * t :] if g == 0 else y[: 2 * r]
+        tokens = y[: B * t] if g == 0 else y[2 * r :]
+        high, low = split(gains[:r] + gains[r:])
+        cols = kgs[g, slot]
+        prod[g] += tokens * cols.astype(F32)
+        proj[g] += dot_nt(cols, high) + dot_nt(cols, low)
 
     def contract(s):
         @pl.when(is_host & (a - s >= 0))
         def _():
-            block(a - s)
+            block(0, a - s)
 
         @pl.when(is_host & (a + s < A))
         def _():
-            block(a + s)
-
-    def pass_rows(first, last):
-        for i in range(first, last):
-
-            @pl.when(has_extra)
-            def _():
-                x_end[i].wait_recv()
-                start(x_extra[i])
-
-            @pl.when(is_end)
-            def _():
-                if i + 1 < CHUNKS:
-                    x_end[i].wait_send()
-                    x_end[i + 1].start()
+            block(0, a + s)
+
+    def pass_rows(i):
+        @pl.when(has_extra)
+        def _():
+            x_end[i].wait_recv()
+            start(x_extra[i])
 
     x = x_ref[...]
     xf = x.astype(F32)
     early[q, :, pl.ds(0, r)] = dot_nt(kg_ref[...], pko_ref[...])
     early[q, :, pl.ds(r, r)] = dot_nt(vg_ref[...], pvo_ref[...])
     early[q, :, pl.ds(3 * r, r)] = dot_nt(x, pdo_ref[...])
-    early[q, :, pl.ds(4 * r, 2 * r)] = jnp.broadcast_to(
-        jnp.sum(xf * xf, axis=1, keepdims=True), (t, 2 * r)
-    )
+    total = jnp.broadcast_to(jnp.sum(xf * xf, axis=1, keepdims=True), (t, 2 * r))
+    squares[q] = jnp.transpose(total)[:8]
+    early_copies = spread(squares, squares_sem, "query", q, Q)
     for load in loads:
         load.wait()
     early[q, :, pl.ds(2 * r, r)] = dot_nt(hid_ref[...], pdi_ref[...])
-    early_copies = spread(early, early_sem, "query", q, Q)
+    early_copies += spread(early, early_sem, "query", q, Q)
     qpg = qpg_ref[...]
     md0 = jnp.sum(xf * gain * qpg.astype(F32), axis=1, keepdims=True) / D
     rg_out = dot_nt(rg_ref[...], pdo_ref[...])
@@ -330,22 +319,10 @@
     def _():
         start(kg_peers)
 
-    forward(1)
-
     @pl.when(is_end)
     def _():
-        for part in range(2):
-
-            @pl.when(has_right)
-            def _():
-                w_copy(wg.at[a, part], a, part, w_right, right).wait_send()
-
-            @pl.when(has_left)
-            def _():
-                w_copy(wg.at[a, part], a, part, w_left, left).wait_send()
-
-        x_end[0].start()
         kg_end.start()
+        start(x_end)
 
     finish(early_copies)
     whole = early[0]
@@ -357,7 +334,11 @@
         limit += jnp.where(place == seq, counts_ref[seq], 0)
     position = lax.rem(f, per_seq) * t + lax.broadcasted_iota(jnp.int32, (t, r), 0)
     mask = jnp.where(position < limit, 1.0, 0.0).astype(F32)
-    inv = lax.rsqrt(whole[:, 4 * r :] / D + 1e-05)
+    total = squares[0]
+    for i in range(1, Q):
+        total = total + squares[i]
+    total = jnp.transpose(jnp.broadcast_to(total[:1], (2 * r, t)))
+    inv = lax.rsqrt(total / D + 1e-05)
     inv_col = inv[:, :1]
     inv_r = inv[:, :r]
     cubed = inv_r * inv_r * inv_r
@@ -374,21 +355,22 @@
     def _():
         pk_end.start()
 
+    forward(1)
+
     @pl.when(has_extra)
     def _():
         kg_end.wait_recv()
         start(kg_extra)
 
-    pass_rows(0, 1)
     normed = (xf * inv_col * gain).astype(BF16)
     attn = dot_nt(normed, pai_ref[...])
     kv_q[q, :, pl.ds(0, r)] = gram(whole[:, :r] * mask, attn)
     kv_q[q, :, pl.ds(r, r)] = gram(whole[:, r : 2 * r] * mask, attn)
     kv_copies = spread(kv_q, kv_q_sem, "query", q, Q)
-    pass_rows(1, 2)
+    pass_rows(0)
     down0 = gram(rg_out + inv_r * qpg_out - back * md0, hidden)
 
-    pass_rows(2, 3)
+    pass_rows(1)
     for copy in kv_copies:
         copy.wait()
     total = kv_q[0]
@@ -396,39 +378,22 @@
         total = total + kv_q[i]
     kv_f[f] = total
     kv_copies = spread(kv_f, kv_f_sem, "fsdp", f, F)
-    pass_rows(3, CHUNKS)
+    @pl.when(is_host)
+    def _():
+        finish(x_pair)
+        finish(kg_peers)
+        block(0, a)
+
+    contract(1)
+    pass_rows(2)
+    forward(2)
+    for i in range(3, CHUNKS):
+        pass_rows(i)
 
     @pl.when(has_extra)
     def _():
         pk_end.wait_recv()
         start(pk_extra)
-
-    forward(2)
-
-    @pl.when(is_end)
-    def _():
-        x_end[CHUNKS - 1].wait_send()
-        kg_end.wait_send()
-        pk_end.wait_send()
-
-    @pl.when(is_host)
-    def _():
-        finish(x_pair)
-        finish(kg_peers)
-        finish(pk_pair)
-
-    @pl.when(has_extra)
-    def _():
-        finish(kg_extra)
-        for copies in x_extra:
-            finish(copies)
-        finish(pk_extra)
-
-    @pl.when(is_host)
-    def _():
-        block(a)
-
-    contract(1)
 
     def step(s, carry):
         forward(s)
@@ -463,13 +428,23 @@
         return totals
 
     lax.fori_loop(3, A - 1, step, 0)
-    for copy in kv_copies:
-        copy.wait()
-    totals = sequences(kv_f)
-    by_query([total[:, :r] for total in totals], 0)
-    by_query([total[:, r:] for total in totals], r * r)
-    scores = score(0, 2 * r * r)
     contract(A - 2)
+
+    @pl.when(is_host)
+    def _():
+        finish(pk_pair)
+
+    def extra_block(slot, carry):
+        block(1, slot)
+        return carry
+
+    @pl.when(has_extra)
+    def _():
+        finish(kg_extra)
+        for copies in x_extra:
+            finish(copies)
+        lax.fori_loop(0, A, extra_block, 0)
+        finish(pk_extra)
 
     d_q[q] = down0
 
@@ -496,17 +471,29 @@
     def drain(slot, carry):
         for part in range(2):
 
-            @pl.when((slot <= a) & has_right & is_host)
+            @pl.when((slot <= a) & has_right & (is_host | (slot == a)))
             def _():
                 w_copy(wg.at[slot, part], slot, part, w_right, right).wait_send()
 
-            @pl.when((slot >= a) & has_left & is_host)
+            @pl.when((slot >= a) & has_left & (is_host | (slot == a)))
             def _():
                 w_copy(wg.at[slot, part], slot, part, w_left, left).wait_send()
 
         return carry
 
     lax.fori_loop(0, A, drain, 0)
+
+    @pl.when(is_end)
+    def _():
+        for copy in [kg_end, pk_end] + x_end:
+            copy.wait_send()
+
+    for copy in kv_copies:
+        copy.wait()
+    totals = sequences(kv_f)
+    by_query([total[:, :r] for total in totals], 0)
+    by_query([total[:, r:] for total in totals], r * r)
+    scores = score(0, 2 * r * r)
     for copy in d_copies:
         copy.wait()
     by_query(sequences(d_f), 2 * r * r)
@@ -577,7 +564,8 @@
             pltpu.VMEM((2 * B * t + 2 * r, d), BF16),
             pltpu.VMEM((B, n, t, 2 * w), BF16),
             pltpu.VMEM((2, A, B * t, 2 * w), BF16),
-            pltpu.VMEM((Q, t, 6 * r), F32),
+            pltpu.VMEM((Q, t, 4 * r), F32),
+            pltpu.VMEM((Q, 8, t), F32),
             pltpu.VMEM((2, B * t, 2 * r), F32),
             pltpu.VMEM((2, B * t, 2 * w), F32),
             pltpu.VMEM((2, B * t, r), F32),
@@ -596,6 +584,7 @@
             dma((2, B)),
             dma((2, Q)),
             dma((2,)),
+            dma((2, Q)),
             dma((2, Q)),
             dma((2, Q)),
             dma((2, B)),

time: 100 us -> 92.4 us (0.924)
  Pallas kernels: 97.1 us -> 89.2 us
    pallas_call x1, Pallas kernels: 97.1 us -> 89.2 us  [shards(): pl.pallas_call(functools.partial(kernel, (F, Q, B, seqs)), out_shape=jax....]
where the time goes in v4:
time: 92.4 us; the launch traced here: 92.2 us
  Pallas kernels  89.2 us (97%)
  local copies, waits for them, and re-layouts  2.4 us (3%)
    pallas_call x1, Pallas kernels, shards(): pl.pallas_call(functools.partial(kernel, (F, Q, B, seqs)), out_shape=jax....  89.2 us

profile of v4, /device:TPU:0, one launch (start us, length us, event | category | flops | bytes accessed | tf_op | source)
XLA Modules:
  0.0 92.2 jit_solution(12265683278087164790)
XLA Ops:
  0.7 1.3 %reshape.3.gain_ref = bf16[1,2048]{1,0:T(2,128)(2,1)} reshape(bf16[2048]{0:T(1024)(128)(2,1)} %param.24) | data formatting | bytes 8192 | tf_op jit(solution)/shard_map/reshape | solution.py:543
  1.9 89.2 %shard_map.154 = f32[1,128]{1,0:T(1,128)} custom-call(bf16[256,2048]{1,0:T(8,128)(2,1)} %x_ref.1, bf16[256,2048]{1,0:T(8,128)(2,1)} %rg_hbm.1, bf16[256,2048]{1,0:T(8,128)(2,1)} %qpg_hbm.1, bf16[256,7168]{1,0:T(8,128)(2,1)} %hid_hbm.1, bf16[256,256]{1,0:T(8,128)(2,1)} %kg_ref.1, bf16[256,256]{1,0:T(8,128)(2,1)} %vg_ref.1, bf16[2048,128]{1,0:T(8,128)(2,1)} %wk_hbm.1, ...), custom_call_target="tpu_custom_call" | custom-call | tf_op jit(solution)/shard_map/pallas_call | solution.py:552
  91.1 1.1 %copy.19 = f32[1,128]{1,0:T(1,128)} copy(f32[1,128]{1,0:T(1,128)} %shard_map.154) | data formatting | bytes 1024

commit v5 on v4

--- a/solution.py
+++ b/solution.py
@@ -9,7 +9,7 @@
 
 D = 8192
 LEN = 2048
-CHUNKS = 4
+CHUNKS = 8
 MESH = pl.DeviceIdType.MESH
 F32 = jnp.float32
 BF16 = jnp.bfloat16
@@ -132,7 +132,7 @@
     ]
     for load in loads:
         load.start()
-    gain = gain_ref[...].astype(F32)
+    gain = gain_ref[...].astype(F32).reshape(1, d)
     own = pl.ds(pl.multiple_of(b * t, t), t)
     xs[own, :] = (x_ref[...].astype(F32) * gain).astype(BF16)
     gp_high, gp_low = split(pdo_ref[...].astype(F32) * gain)
@@ -367,10 +367,12 @@
     kv_q[q, :, pl.ds(0, r)] = gram(whole[:, :r] * mask, attn)
     kv_q[q, :, pl.ds(r, r)] = gram(whole[:, r : 2 * r] * mask, attn)
     kv_copies = spread(kv_q, kv_q_sem, "query", q, Q)
-    pass_rows(0)
+    for i in range(2):
+        pass_rows(i)
     down0 = gram(rg_out + inv_r * qpg_out - back * md0, hidden)
 
-    pass_rows(1)
+    for i in range(2, 4):
+        pass_rows(i)
     for copy in kv_copies:
         copy.wait()
     total = kv_q[0]
@@ -378,6 +380,8 @@
         total = total + kv_q[i]
     kv_f[f] = total
     kv_copies = spread(kv_f, kv_f_sem, "fsdp", f, F)
+    pass_rows(4)
+
     @pl.when(is_host)
     def _():
         finish(x_pair)
@@ -385,10 +389,9 @@
         block(0, a)
 
     contract(1)
-    pass_rows(2)
+    for i in range(5, CHUNKS):
+        pass_rows(i)
     forward(2)
-    for i in range(3, CHUNKS):
-        pass_rows(i)
 
     @pl.when(has_extra)
     def _():
@@ -540,7 +543,7 @@
         (value_grad, vmem),
         (key_weight, hbm),
         (value_weight, hbm),
-        (norm_gain.reshape(1, d), vmem),
+        (norm_gain, vmem),
         (proj_attn_in, vmem),
         (proj_key_out, vmem),
         (proj_value_out, vmem),

time: 92.4 us -> 89.7 us (0.971)
  Pallas kernels: 89.2 us -> 87.7 us
  local copies, waits for them, and re-layouts: 2.4 us -> 1.19 us
    pallas_call x1, Pallas kernels: 89.2 us -> 87.7 us  [shards(): pl.pallas_call(functools.partial(kernel, (F, Q, B, seqs)), out_shape=jax....]
    reshape x1 -> x0, local copies, waits for them, and re-layouts: 1.29 us -> none  [shards(): norm_gain.reshape(1, d)]
where the time goes in v5:
time: 89.7 us; the launch traced here: 89.5 us
  Pallas kernels  87.7 us (98%)
  local copies, waits for them, and re-layouts  1.19 us (1%)
    pallas_call x1, Pallas kernels, shards(): pl.pallas_call(functools.partial(kernel, (F, Q, B, seqs)), out_shape=jax....  87.7 us

profile of v5, /device:TPU:0, one launch (start us, length us, event | category | flops | bytes accessed | tf_op | source)
XLA Modules:
  0.0 89.5 jit_solution(3221211637047907903)
XLA Ops:
  0.7 87.7 %shard_map.154 = f32[1,128]{1,0:T(1,128)} custom-call(bf16[256,2048]{1,0:T(8,128)(2,1)} %x_ref.1, bf16[256,2048]{1,0:T(8,128)(2,1)} %rg_hbm.1, bf16[256,2048]{1,0:T(8,128)(2,1)} %qpg_hbm.1, bf16[256,7168]{1,0:T(8,128)(2,1)} %hid_hbm.1, bf16[256,256]{1,0:T(8,128)(2,1)} %kg_ref.1, bf16[256,256]{1,0:T(8,128)(2,1)} %vg_ref.1, bf16[2048,128]{1,0:T(8,128)(2,1)} %wk_hbm.1, ...), custom_call_target="tpu_custom_call" | custom-call | tf_op jit(solution)/shard_map/pallas_call | solution.py:555
  88.3 1.2 %copy.19 = f32[1,128]{1,0:T(1,128)} copy(f32[1,128]{1,0:T(1,128)} %shard_map.154) | data formatting | bytes 1024
